TPU v7x, 32 devices: a whole 2x2x4 slice. The times are simulated.
32 devices in a mesh: ctx: 8 (over z, y), tp: 4 (over x, core).
Axes of the slice: x: 2, y: 2, z: 4, core: 2. Of those that a mesh axis runs over, the one named last changes fastest.
Arguments:
- stream_in: bfloat16 [8192, 4096], P('ctx', 'tp'), may hold values from -12 to 12
- features: bfloat16 [8192, 3, 4096], P('ctx', None, 'tp'), may hold values from -6 to 6
- mr_taps: float32 [3, 4096, 7], P(None, 'tp'), may hold values from -2 to 2
- mr_filter: bfloat16 [4096, 128], P('tp'), may hold values from -0.5 to 0.5
- norm_gain: float32 [4096], P('tp'), may hold values from 0.1 to 1.9
- li_taps: float32 [3, 4096, 7], P(None, 'tp'), may hold values from -2 to 2
- modal_rates: float32 [4096, 16], P('tp'), may hold values from 2.4414062e-06 to 0.1
- modal_weights: float32 [4096, 16], P('tp'), may hold values from -1.5 to 1.5
Outputs:
- mixed: bfloat16 [8192, 4096], P('ctx', 'tp')
All inputs are finite; a program needn't handle non-finite values.
Results may differ from a plain program's by a relative error of at most 0.015.
Values may be sent and summed in bfloat16 or wider, within the bound.
A program may use at most 256 MiB of HBM per device.

v0:
```python
import functools

import jax
import jax.numpy as jnp
import ml_dtypes
import numpy as np
from jax import lax
from jax.experimental import pallas as pl
from jax.experimental.pallas import tpu as pltpu
from jax.sharding import PartitionSpec as P

EPS = 1e-06
MODES = 16
TAPS = 7
MR = 128
HALO = 144
LEAD = 8
SEGS = 8
NFFT = 512
HALF = NFFT // 2
FIRST = HALO - LEAD
VMEM_LIMIT = 60 * 1024 * 1024
f32 = jnp.float32
bf16 = jnp.bfloat16


def split_np(matrix):
    high = matrix.astype(np.float32).astype(ml_dtypes.bfloat16)
    low = (matrix - high.astype(np.float64)).astype(np.float32).astype(ml_dtypes.bfloat16)
    return high, low


def dft_tables(out_rows):
    k = np.arange(HALF)[:, None]
    i = np.arange(NFFT)[None, :]
    angle = 2.0 * np.pi * ((k * i) % NFFT) / NFFT
    sign = 1.0 - 2.0 * (i % 2)
    forward = np.concatenate([np.cos(angle), -np.sin(angle)], axis=0)
    forward[HALF] = sign[0]
    back = 2.0 * forward.T / NFFT
    back[:, 0] *= 0.5
    back[:, HALF] *= 0.5
    return split_np(forward), split_np(back[FIRST : FIRST + out_rows])


def steps(count, unroll, step, carry):
    main = count // unroll
    carry = lax.fori_loop(0, main, lambda it, c: step(it * unroll, unroll, c), carry)
    if count % unroll:
        carry = step(main * unroll, count % unroll, carry)
    return carry


def tree(terms):
    while len(terms) > 1:
        terms = [sum(terms[i + 1 : i + 2], terms[i]) for i in range(0, len(terms), 2)]
    return terms[0]


def first_kernel(
    rows, win, wins, begin, feat, halo, stream, taps, filt, fh, fl, g_mat, out, sq, xs, prod, gate
):
    low_row = 8 if begin == 0 else begin
    last = (begin // win + wins - 1) * win
    high = min(HALO + rows, last + FIRST + win if begin == 0 else HALO + rows)
    base_x = low_row - 8
    seg = (high - low_row) // SEGS
    tail = last + NFFT

    for g in range(2):
        lanes = slice(g * 128, g * 128 + 128)
        if begin == 0:
            own = high - HALO
            own16 = -(-own // 16) * 16
            for f in range(3):
                xs[f, HALO : HALO + own16, :] = feat[f, 0:own16, lanes].astype(f32)
            xs[0, HALO - 16 : HALO, :] = halo[2 * HALO : 2 * HALO + 16, lanes].astype(f32)
            xs[1, 0:HALO, :] = halo[0:HALO, lanes].astype(f32)
            xs[2, 0:HALO, :] = halo[HALO : 2 * HALO, lanes].astype(f32)
            shift = 0
        else:
            skip = (base_x - HALO) // 16 * 16
            shift = base_x - HALO - skip
            for f in range(3):
                xs[f, 0 : rows - skip, :] = feat[f, skip:rows, lanes].astype(f32)

        def step(t0, n, carry):
            made = []
            for f in range(3):
                held = [xs[f, pl.ds(t0 + j + 2 + shift, SEGS, stride=seg), :] for j in range(n + 6)]
                ws = [taps[f, k : k + 1, lanes] for k in range(TAPS)]
                made.append([tree([ws[k] * held[u + 6 - k] for k in range(TAPS)]) for u in range(n)])
            for u in range(n):
                at = pl.ds(t0 + u + low_row - begin, SEGS, stride=seg)
                prod[g, at, :] = made[1][u] * made[2][u]
                gate[g, at, :] = made[0][u]
            return carry

        steps(seg, 6, step, 0)
        if low_row > begin:
            prod[g, 0 : low_row - begin, :] = jnp.zeros((low_row - begin, 128), f32)
        if tail > high:
            prod[g, high - begin : tail - begin, :] = jnp.zeros((tail - high, 128), f32)

    nt = (((1,), (1,)), ((), ()))
    spec = lax.dot_general(fh[:, 0:MR], filt[...], nt, preferred_element_type=f32)
    spec = spec + lax.dot_general(fl[:, 0:MR], filt[...], nt, preferred_element_type=f32)
    hr, hi = spec[:HALF], spec[HALF:]
    top = lax.broadcasted_iota(jnp.int32, hr.shape, 0) == 0
    mid = jnp.where(top, 0.0, hi)
    low = jnp.where(top, hi, hr)

    for b in range(wins):
        start = win * b
        x = jnp.concatenate(
            [prod[0, start : start + NFFT, :], prod[1, start : start + NFFT, :]], axis=1
        ).astype(bf16)
        s = jnp.dot(fh[...], x, preferred_element_type=f32)
        sr, si = s[:HALF], s[HALF:]
        y = jnp.concatenate(
            [(hr * sr - mid * si).astype(bf16), (mid * sr + low * si).astype(bf16)], axis=0
        )
        medium = jnp.dot(g_mat[...], y, preferred_element_type=f32)[:win]
        first = FIRST + start
        gates = jnp.concatenate(
            [gate[0, first : first + win, :], gate[1, first : first + win, :]], axis=1
        )
        if begin == 0 and b == 0:
            head = halo[2 * HALO + 16 : 2 * HALO + 32, :].astype(f32)[16 - LEAD :]
            base = jnp.concatenate([head, stream[0 : win - LEAD, :].astype(f32)], axis=0)
        else:
            base = stream[begin + start - LEAD : begin + start - LEAD + win, :].astype(f32)
        value = base + gates * medium
        out[start : start + win, :] = value
        squared = value * value
        part = squared[:, :128] + squared[:, 128:]

        @pl.when(pl.program_id(0) == 0)
        def _():
            sq[start : start + win, :] = part

        @pl.when(pl.program_id(0) > 0)
        def _():
            sq[start : start + win, :] = sq[start : start + win, :] + part


def second_kernel(
    seg, count, lanes_count, whole, near, far, near_sq, far_sq, gain, taps, rates,
    prod, gate, states, gathered, nrm, held_total, send_sem, recv_sem,
    parts, sums, scale, sum_send, sum_recv, decay,
):
    n = seg * SEGS
    me = lax.axis_index("ctx")
    group = pl.program_id(0)
    groups = held_total.shape[0]

    def peer_copy(g, k):
        return pltpu.make_async_remote_copy(
            src_ref=held_total.at[g],
            dst_ref=gathered.at[g, me],
            send_sem=send_sem.at[g, k - 1],
            recv_sem=recv_sem.at[g, k - 1],
            device_id={"ctx": lax.rem(me + k, count)},
            device_id_type=pl.DeviceIdType.MESH,
        )

    @pl.when(group == 0)
    def _():
        barrier = pltpu.get_barrier_semaphore()

        def greet(k, c):
            pl.semaphore_signal(
                barrier, inc=1, device_id={"ctx": lax.rem(me + k, count)},
                device_id_type=pl.DeviceIdType.MESH,
            )
            return c

        lax.fori_loop(1, count, greet, 0)
        mine = lax.axis_index("tp")
        for k in range(1, lanes_count):
            pl.semaphore_signal(
                barrier, inc=1, device_id={"tp": lax.rem(mine + k, lanes_count)},
                device_id_type=pl.DeviceIdType.MESH,
            )
        pl.semaphore_wait(barrier, count - 1 + lanes_count - 1)

        half = near_sq.shape[0]
        scale[0:half, :] = near_sq[...]
        scale[half:n, :] = far_sq[...]
        scale[n:, :] = jnp.zeros((scale.shape[0] - n, 128), f32)
        parts[0] = lax.dot_general(
            jnp.ones((8, 128), f32), scale[...], (((1,), (1,)), ((), ())),
            precision=lax.Precision.HIGHEST, preferred_element_type=f32,
        )
        copies = [
            pltpu.make_async_remote_copy(
                src_ref=parts.at[0],
                dst_ref=parts.at[k],
                send_sem=sum_send.at[k - 1],
                recv_sem=sum_recv.at[k - 1],
                device_id={"tp": lax.rem(mine + k, lanes_count)},
                device_id_type=pl.DeviceIdType.MESH,
            )
            for k in range(1, lanes_count)
        ]
        for copy in copies:
            copy.start()
        for copy in copies:
            copy.wait()
        sums[...] = parts[0]
        for k in range(1, lanes_count):
            sums[...] = sums[...] + parts[k]
        column = lax.dot_general(
            sums[...], jnp.full((8, 128), 0.125, f32), (((0,), (0,)), ((), ())),
            precision=lax.Precision.HIGHEST, preferred_element_type=f32,
        )
        scale[...] = lax.rsqrt(column / whole + EPS)

    cut = near.shape[0]
    nrm[0:8, :] = jnp.zeros((8, 128), f32)
    nrm[8 : 8 + cut, :] = (near[...] * scale[0:cut, :] * gain[...]).astype(bf16).astype(f32)
    nrm[8 + cut : 8 + n, :] = (far[...] * scale[cut:n, :] * gain[...]).astype(bf16).astype(f32)
    place = lax.broadcasted_iota(jnp.int32, (SEGS, 128), 0) * seg
    left = ((SEGS - 1) * seg - place).astype(f32)
    decay[...] = jnp.exp(-rates[...])

    def step(t0, size, state):
        held = [nrm[pl.ds(t0 + j + 2, SEGS, stride=seg), :] for j in range(size + 6)]
        state = list(state)
        made = []
        for f in range(3):
            ws = [taps[f, k : k + 1, :] for k in range(TAPS)]
            made.append([tree([ws[k] * held[u + 6 - k] for k in range(TAPS)]) for u in range(size)])
        values = []
        for u in range(size):
            p = (made[1][u] * made[2][u]).astype(bf16).astype(f32)
            p = jnp.where(place + (t0 + u) >= LEAD, p, 0.0)
            prod[t0 + u] = p
            gate[t0 + u] = made[0][u]
            values.append(p)
        for m in range(MODES):
            d = decay[m : m + 1, :]
            for u in range(size):
                state[m] = state[m] * d + values[u]
        return tuple(state)

    zero = jnp.zeros((SEGS, 128), f32)
    state = steps(seg, 6, step, (zero,) * MODES)
    for m in range(MODES):
        states[m] = state[m]
        held_total[group, m : m + 1, :] = jnp.sum(
            state[m] * jnp.exp(-rates[m : m + 1, :] * left), axis=0, keepdims=True
        )

    def send(k, c):
        @pl.when(me + k < count)
        def _():
            peer_copy(group, k).start()

        return c

    lax.fori_loop(1, count, send, 0)

    @pl.when(group == groups - 1)
    def _():
        def finish(at, c):
            g, k = at // (count - 1), at % (count - 1) + 1

            @pl.when(me + k < count)
            def _():
                peer_copy(g, k).wait_send()

            @pl.when(me - k >= 0)
            def _():
                peer_copy(g, k).wait_recv()

            return c

        lax.fori_loop(0, groups * (count - 1), finish, 0)


def third_kernel(
    seg, count, prod, gate, states, totals, lags, near, far, rates, weight, out, init, ybuf, decay
):
    n = seg * SEGS
    r = rates[...]
    decay[...] = jnp.exp(-r)
    span = jnp.exp(-r * seg)
    row = jnp.zeros(r.shape, f32)
    for e in range(count):
        lag = lags[e : e + 1, :]
        used = jnp.broadcast_to(lag, r.shape) > -2.0 * LEAD
        coef = jnp.exp(-r * jnp.maximum(lag, float(-LEAD)))
        row = row + jnp.where(used, coef * totals[0, e], 0.0)
    for s in range(SEGS):
        init[:, s, :] = row
        row = row * span + states[:, s, :]

    def step(t0, size, state):
        state = list(state)
        values = [prod[t0 + u] for u in range(size)]
        sums = [[None] * 2 for _ in range(size)]
        for m in range(MODES):
            d = decay[m : m + 1, :]
            w = weight[m : m + 1, :]
            for u in range(size):
                state[m] = state[m] * d + values[u]
                term = state[m] * w
                had = sums[u][m % 2]
                sums[u][m % 2] = term if had is None else had + term
        for u in range(size):
            ybuf[pl.ds(t0 + u, SEGS, stride=seg), :] = gate[t0 + u] * (sums[u][0] + sums[u][1])
        return tuple(state)

    steps(seg, 8, step, tuple(init[m] for m in range(MODES)))
    cut = near.shape[0]
    out[0 : cut - LEAD, :] = (near[LEAD:cut, :] + ybuf[LEAD:cut, :]).astype(bf16)
    out[cut - LEAD : n - LEAD, :] = (far[...] + ybuf[cut:n, :]).astype(bf16)


def params(**more):
    return pltpu.CompilerParams(
        dimension_semantics=("arbitrary",), vmem_limit_bytes=VMEM_LIMIT, **more
    )


def body(stream_in, features, mr_taps, mr_filter, norm_gain, li_taps, modal_rates, modal_weights):
    rows, _, width = features.shape
    count = lax.axis_size("ctx")
    place = lax.axis_index("ctx")
    whole = width * lax.axis_size("tp")
    ext = rows + LEAD
    feats = jnp.transpose(features, (1, 0, 2))
    taps_one = jnp.transpose(mr_taps, (0, 2, 1))
    taps_two = jnp.transpose(li_taps, (0, 2, 1))
    rates = jnp.transpose(modal_rates)
    weights = jnp.transpose(modal_weights)

    tail = jnp.concatenate(
        [
            feats[1, rows - HALO :],
            feats[2, rows - HALO :],
            feats[0, rows - 16 :],
            stream_in[rows - 16 :],
        ],
        axis=0,
    )
    halo = lax.ppermute(tail, "ctx", [(i, i + 1) for i in range(count - 1)])

    wins = next(w for w in range(1, ext) if ext % w == 0 and (ext // w) % 8 == 0 and ext // w + FIRST <= NFFT)
    win = ext // wins
    padded = -(-win // 16) * 16
    (fh, fl), (gh, gl) = dft_tables(padded)
    cb = 256
    full = lambda shape: pl.BlockSpec(shape, lambda j: (0,) * len(shape))
    fh, fl, g_mat = jnp.asarray(fh), jnp.asarray(fl), jnp.asarray(gh)

    def medium(begin, count_wins, halo):
        out_rows = win * count_wins
        buf = max(HALO + rows - begin, (count_wins - 1) * win + NFFT)
        return pl.pallas_call(
            functools.partial(first_kernel, rows, win, count_wins, begin),
            grid=(width // cb,),
            in_specs=[
                pl.BlockSpec((3, rows, cb), lambda j: (0, 0, j)),
                pl.BlockSpec((halo.shape[0], cb), lambda j: (0, j)),
                pl.BlockSpec((rows, cb), lambda j: (0, j)),
                pl.BlockSpec((3, TAPS, cb), lambda j: (0, 0, j)),
                pl.BlockSpec((cb, MR), lambda j: (j, 0)),
                full((NFFT, NFFT)),
                full((NFFT, NFFT)),
                full((padded, NFFT)),
            ],
            out_specs=[
                pl.BlockSpec((out_rows, cb), lambda j: (0, j)),
                pl.BlockSpec((out_rows, 128), lambda j: (0, 0)),
            ],
            out_shape=[
                jax.ShapeDtypeStruct((out_rows, width), f32),
                jax.ShapeDtypeStruct((out_rows, 128), f32),
            ],
            scratch_shapes=[
                pltpu.VMEM((3, HALO + rows, 128), f32),
                pltpu.VMEM((2, buf, 128), f32),
                pltpu.VMEM((2, buf, 128), f32),
            ],
            compiler_params=params(),
            cost_estimate=pl.CostEstimate(
                flops=12_000_000_000 * count_wins, bytes_accessed=20_000_000 * count_wins, transcendentals=0
            ),
            name="medium_head" if begin == 0 else "medium_rest",
        )(feats, halo, stream_in, taps_one, mr_filter, fh, fl, g_mat)

    far, far_squares = medium(win, wins - 1, stream_in[:16])
    near, near_squares = medium(0, 1, halo)
    seg = ext // SEGS
    lanes_count = lax.axis_size("tp")
    scaled = weights * jnp.sqrt(-jnp.expm1(-2.0 * rates))
    apart = place - 1 - jnp.arange(count)
    lags = jnp.where(apart >= 0, apart * rows - LEAD, -4 * LEAD).astype(f32)
    lags = jnp.broadcast_to(lags[:, None], (count, 128))
    summed = -(-ext // 128) * 128
    col = lambda *lead: pl.BlockSpec(lead + (128,), lambda j: (0,) * len(lead) + (j,))
    groups = width // 128
    prod, gate, states, totals = pl.pallas_call(
        functools.partial(second_kernel, seg, count, lanes_count, whole),
        grid=(width // 128,),
        in_specs=[
            col(win),
            col(ext - win),
            full((win, 128)),
            full((ext - win, 128)),
            col(1),
            col(3, TAPS),
            col(MODES),
        ],
        out_specs=[col(seg, SEGS), col(seg, SEGS), col(MODES, SEGS), pl.BlockSpec(memory_space=pl.ANY)],
        out_shape=[
            jax.ShapeDtypeStruct((seg, SEGS, width), f32),
            jax.ShapeDtypeStruct((seg, SEGS, width), f32),
            jax.ShapeDtypeStruct((MODES, SEGS, width), f32),
            jax.ShapeDtypeStruct((groups, count, MODES, 128), f32),
        ],
        scratch_shapes=[
            pltpu.VMEM((8 + ext, 128), f32),
            pltpu.VMEM((groups, MODES, 128), f32),
            pltpu.SemaphoreType.DMA((groups, count - 1)),
            pltpu.SemaphoreType.DMA((groups, count - 1)),
            pltpu.VMEM((lanes_count, 8, summed), f32),
            pltpu.VMEM((8, summed), f32),
            pltpu.VMEM((summed, 128), f32),
            pltpu.SemaphoreType.DMA((lanes_count - 1,)),
            pltpu.SemaphoreType.DMA((lanes_count - 1,)),
            pltpu.VMEM((MODES, 128), f32),
        ],
        compiler_params=params(collective_id=0, has_side_effects=True),
        name="states",
    )(near, far, near_squares, far_squares, norm_gain[None, :], taps_two, rates)

    return pl.pallas_call(
        functools.partial(third_kernel, seg, count),
        grid=(width // 128,),
        in_specs=[
            col(seg, SEGS),
            col(seg, SEGS),
            col(MODES, SEGS),
            pl.BlockSpec((1, count, MODES, 128), lambda j: (j, 0, 0, 0)),
            full((count, 128)),
            col(win),
            col(ext - win),
            col(MODES),
            col(MODES),
        ],
        out_specs=col(rows),
        out_shape=jax.ShapeDtypeStruct((rows, width), bf16),
        scratch_shapes=[pltpu.VMEM((MODES, SEGS, 128), f32), pltpu.VMEM((ext, 128), f32), pltpu.VMEM((MODES, 128), f32)],
        compiler_params=params(),
        name="mix",
    )(prod, gate, states, totals, lags, near, far, rates, scaled)


def solution(mesh):
    in_specs = (
        P("ctx", "tp"),
        P("ctx", None, "tp"),
        P(None, "tp", None),
        P("tp", None),
        P("tp"),
        P(None, "tp", None),
        P("tp", None),
        P("tp", None),
    )
    return jax.shard_map(
        body, mesh=mesh, in_specs=in_specs, out_specs=P("ctx", "tp"), check_vma=False
    )
```

profile of v0, /device:TPU:24, one launch (start us, length us, event | category | flops | bytes accessed | tf_op | source)
XLA Modules:
  0.0 77.9 jit_solution(277366457820496570)
XLA Ops:
  0.0 0.8 slice_bitcast_fusion.2
  0.8 1.1 %slice_bitcast_fusion.1 = (bf16[144,1024]{1,0:T(8,128)(2,1)S(1)}, bf16[144,1024]{1,0:T(8,128)(2,1)S(1)}) fusion(bf16[3,1024,1024]{2,1,0:T(8,128)(2,1)} %bitcast.18), kind=kLoop, calls=%fused_computation.2 | loop fusion | bytes 1179648 | tf_op jit(solution)/shard_map/squeeze | solution.py:341
  1.9 1.4 %fusion.1 = (bf16[16,1024]{1,0:T(8,128)(2,1)}, bf16[16,1024]{1,0:T(8,128)(2,1)S(1)}) fusion(bf16[1024,1024]{1,0:T(8,128)(2,1)} %stream.3), kind=kLoop, calls=%fused_computation.7 | loop fusion | bytes 131072 | tf_op jit(solution)/shard_map/slice | solution.py:394
  3.3 3.4 %collective-permute-start = (bf16[320,1024]{1,0:T(8,128)(2,1)S(1)}, bf16[320,1024]{1,0:T(8,128)(2,1)S(1)}, u32[]{:S(2)}, u32[]{:S(2)}) collective-permute-start(bf16[320,1024]{1,0:T(8,128)(2,1)S(1)} %pad_maximum_fusion), channel_id=1, source_target_pairs={{0,4},{4,8},{8,12},{12,16},{16,20},{20,24},{24,28},{1,5},{5,9},{9,... | collective-permute-start | bytes 1966088 | tf_op jit(solution)/shard_map/ppermute | solution.py:348
  6.7 0.0 copy-start
  6.7 0.0 copy-start.1
  6.8 15.4 %medium_rest.1 = (f32[688,1024]{1,0:T(8,128)}, f32[688,128]{1,0:T(8,128)}) custom-call(bf16[3,1024,1024]{2,1,0:T(8,128)(2,1)} %bitcast.19, bf16[16,1024]{1,0:T(8,128)(2,1)} %get-tuple-element.23.halo, bf16[1024,1024]{1,0:T(8,128)(2,1)} %stream.3, f32[3,7,1024]{2,1,0:T(8,128)} %bitcast.22, bf16[1024,128]{1,0:T(8,128)(2,1)} %filt.3, ...), custom_call_target="tpu_custom_call" | custom-call | flops 24000000000 | bytes 40000000 | tf_op jit(solution)/shard_map/medium_rest/pallas_call | solution.py:361
  22.2 0.0 copy-done
  22.2 0.0 copy-done.1
  22.2 0.7 bitcast_multiply_fusion.weight
  22.8 0.0 collective-permute-done.halo
  22.8 0.0 copy-start.2
  22.8 0.8 %copy-done.2 = bf16[320,1024]{1,0:T(8,128)(2,1)} copy-done((bf16[320,1024]{1,0:T(8,128)(2,1)}, bf16[320,1024]{1,0:T(8,128)(2,1)S(1)}, u32[]{:S(2)}) %copy-start.2) | copy-done | bytes 655384
  23.7 9.9 %medium_head.1 = (f32[344,1024]{1,0:T(8,128)}, f32[344,128]{1,0:T(8,128)}) custom-call(bf16[3,1024,1024]{2,1,0:T(8,128)(2,1)} %bitcast.20, bf16[320,1024]{1,0:T(8,128)(2,1)} %copy-done.2, bf16[1024,1024]{1,0:T(8,128)(2,1)} %stream.3, f32[3,7,1024]{2,1,0:T(8,128)} %bitcast.23, bf16[1024,128]{1,0:T(8,128)(2,1)} %filt.3, bf16[512,512]{1,0:T(8,128)(2,1)} %constant.26.clone.fh, ...), custom_call_target="tpu_custom_call" | custom-call | flops 12000000000 | bytes 20000000 | tf_op jit(solution)/shard_map/medium_head/pallas_call | solution.py:361
  33.5 29.8 %states.1 = (f32[129,8,1024]{2,1,0:T(8,128)}, f32[129,8,1024]{2,1,0:T(8,128)}, f32[16,8,1024]{2,1,0:T(8,128)}, f32[8,8,16,128]{3,2,1,0:T(8,128)}) custom-call(f32[344,1024]{1,0:T(8,128)} %get-tuple-element.13.near, f32[688,1024]{1,0:T(8,128)} %get-tuple-element.14.far, f32[344,128]{1,0:T(8,128)} %get-tuple-element.15.near_sq, ...), custom_call_target="tpu_custom_call" | custom-call | tf_op jit(solution)/shard_map/states/pallas_call | solution.py:405
  63.4 0.7 broadcast_in_dim.15.lags
  64.1 13.8 %mix.1 = bf16[1024,1024]{1,0:T(8,128)(2,1)} custom-call(f32[129,8,1024]{2,1,0:T(8,128)} %get-tuple-element.17.prod, f32[129,8,1024]{2,1,0:T(8,128)} %get-tuple-element.18.gate, f32[16,8,1024]{2,1,0:T(8,128)} %get-tuple-element.19.states, f32[8,8,16,128]{3,2,1,0:T(8,128)} %get-tuple-element.20.totals, f32[8,128]{1,0:T(8,128)} %broadcast_in_dim.15.lags, ...), custom_call_target="tpu_custom_call" | custom-call | tf_op jit(solution)/shard_map/mix/pallas_call | solution.py:440
  (2 shorter events, 0.1 us)
Async XLA Ops:
  3.3 19.5 %collective-permute-start = (bf16[320,1024]{1,0:T(8,128)(2,1)S(1)}, bf16[320,1024]{1,0:T(8,128)(2,1)S(1)}, u32[]{:S(2)}, u32[]{:S(2)}) collective-permute-start(bf16[320,1024]{1,0:T(8,128)(2,1)S(1)} %pad_maximum_fusion), channel_id=1, source_target_pairs={{0,4},{4,8},{8,12},{12,16},{16,20},{20,24},{24,28},{1,5},{5,9},{9,... | collective-permute-start | bytes 1966088 | tf_op jit(solution)/shard_map/ppermute | solution.py:348
  6.7 15.4 %copy-start = (f32[1024,16]{0,1:T(8,128)S(1)}, f32[1024,16]{0,1:T(8,128)}, u32[]{:S(2)}) copy-start(f32[1024,16]{0,1:T(8,128)} %param.17) | copy-start | bytes 196612
  6.7 15.4 %copy-start.1 = (f32[1024,16]{0,1:T(8,128)S(1)}, f32[1024,16]{0,1:T(8,128)}, u32[]{:S(2)}) copy-start(f32[1024,16]{0,1:T(8,128)} %param.18) | copy-start | bytes 196612
  22.8 0.8 %copy-start.2 = (bf16[320,1024]{1,0:T(8,128)(2,1)}, bf16[320,1024]{1,0:T(8,128)(2,1)S(1)}, u32[]{:S(2)}) copy-start(bf16[320,1024]{1,0:T(8,128)(2,1)S(1)} %collective-permute-done.halo) | copy-start | bytes 1966084
where the time goes:
time: 78.5 us; the launch traced here: 77.9 us
  Pallas kernels  68.9 us (88%)
  local copies, waits for them, and re-layouts  4.75 us (6%)
  starting transfers between devices  3.43 us (4%)
    pallas_call x1, Pallas kernels, body(): pl.pallas_call(functools.partial(second_kernel, seg, count, lanes_count,...  29.8 us
    pallas_call x2, Pallas kernels, medium(): pl.pallas_call(functools.partial(first_kernel, rows, win, count_wins, beg...  25.3 us
    pallas_call x1, Pallas kernels, body(): pl.pallas_call(functools.partial(third_kernel, seg, count), grid=(width /...  13.8 us
    ppermute x1, starting transfers between devices, body(): halo = lax.ppermute(tail, 'ctx', [(i, i + 1) for i in range(count - 1)])  3.43 us
  transfers between devices with their start and end apart: 1, of which 0 were waited for; matrix products, arithmetic and copies ran while one was open for 1% of the time, Pallas kernels for 20%

commit v1 on v0

--- a/solution.py
+++ b/solution.py
@@ -55,6 +55,24 @@
     while len(terms) > 1:
         terms = [sum(terms[i + 1 : i + 2], terms[i]) for i in range(0, len(terms), 2)]
     return terms[0]
+
+
+def tail_kernel(rows, feats, stream, out, sems):
+    copies = [
+        pltpu.make_async_copy(source, out.at[place : place + size, :], sems.at[i])
+        for i, (source, place, size) in enumerate(
+            [
+                (feats.at[1, rows - HALO : rows, :], 0, HALO),
+                (feats.at[2, rows - HALO : rows, :], HALO, HALO),
+                (feats.at[0, rows - 16 : rows, :], 2 * HALO, 16),
+                (stream.at[rows - 16 : rows, :], 2 * HALO + 16, 16),
+            ]
+        )
+    ]
+    for copy in copies:
+        copy.start()
+    for copy in copies:
+        copy.wait()
 
 
 def first_kernel(
@@ -96,7 +114,7 @@
                 gate[g, at, :] = made[0][u]
             return carry
 
-        steps(seg, 6, step, 0)
+        steps(seg, 12, step, 0)
         if low_row > begin:
             prod[g, 0 : low_row - begin, :] = jnp.zeros((low_row - begin, 128), f32)
         if tail > high:
@@ -280,18 +298,19 @@
 
 
 def third_kernel(
-    seg, count, prod, gate, states, totals, lags, near, far, rates, weight, out, init, ybuf, decay
+    seg, count, prod, gate, states, totals, near, far, rates, weight, out, init, ybuf, decay
 ):
     n = seg * SEGS
+    rows = n - LEAD
+    me = lax.axis_index("ctx")
     r = rates[...]
     decay[...] = jnp.exp(-r)
     span = jnp.exp(-r * seg)
     row = jnp.zeros(r.shape, f32)
     for e in range(count):
-        lag = lags[e : e + 1, :]
-        used = jnp.broadcast_to(lag, r.shape) > -2.0 * LEAD
-        coef = jnp.exp(-r * jnp.maximum(lag, float(-LEAD)))
-        row = row + jnp.where(used, coef * totals[0, e], 0.0)
+        apart = jnp.full(r.shape, me - 1 - e, jnp.int32)
+        coef = jnp.exp(-r * (jnp.maximum(apart, 0) * rows - LEAD).astype(f32))
+        row = row + jnp.where(apart >= 0, coef * totals[0, e], 0.0)
     for s in range(SEGS):
         init[:, s, :] = row
         row = row * span + states[:, s, :]
@@ -327,7 +346,6 @@
 def body(stream_in, features, mr_taps, mr_filter, norm_gain, li_taps, modal_rates, modal_weights):
     rows, _, width = features.shape
     count = lax.axis_size("ctx")
-    place = lax.axis_index("ctx")
     whole = width * lax.axis_size("tp")
     ext = rows + LEAD
     feats = jnp.transpose(features, (1, 0, 2))
@@ -336,15 +354,16 @@
     rates = jnp.transpose(modal_rates)
     weights = jnp.transpose(modal_weights)
 
-    tail = jnp.concatenate(
-        [
-            feats[1, rows - HALO :],
-            feats[2, rows - HALO :],
-            feats[0, rows - 16 :],
-            stream_in[rows - 16 :],
-        ],
-        axis=0,
-    )
+    anywhere = pl.BlockSpec(memory_space=pl.ANY)
+    tail = pl.pallas_call(
+        functools.partial(tail_kernel, rows),
+        in_specs=[anywhere, anywhere],
+        out_specs=anywhere,
+        out_shape=jax.ShapeDtypeStruct((2 * HALO + 32, width), bf16),
+        scratch_shapes=[pltpu.SemaphoreType.DMA((4,))],
+        compiler_params=pltpu.CompilerParams(vmem_limit_bytes=VMEM_LIMIT),
+        name="tail",
+    )(feats, stream_in)
     halo = lax.ppermute(tail, "ctx", [(i, i + 1) for i in range(count - 1)])
 
     wins = next(w for w in range(1, ext) if ext % w == 0 and (ext // w) % 8 == 0 and ext // w + FIRST <= NFFT)
@@ -358,13 +377,14 @@
     def medium(begin, count_wins, halo):
         out_rows = win * count_wins
         buf = max(HALO + rows - begin, (count_wins - 1) * win + NFFT)
+        need = 512 if begin == 0 and rows % 512 == 0 else rows
         return pl.pallas_call(
             functools.partial(first_kernel, rows, win, count_wins, begin),
             grid=(width // cb,),
             in_specs=[
-                pl.BlockSpec((3, rows, cb), lambda j: (0, 0, j)),
+                pl.BlockSpec((3, need, cb), lambda j: (0, 0, j)),
                 pl.BlockSpec((halo.shape[0], cb), lambda j: (0, j)),
-                pl.BlockSpec((rows, cb), lambda j: (0, j)),
+                pl.BlockSpec((need, cb), lambda j: (0, j)),
                 pl.BlockSpec((3, TAPS, cb), lambda j: (0, 0, j)),
                 pl.BlockSpec((cb, MR), lambda j: (j, 0)),
                 full((NFFT, NFFT)),
@@ -396,9 +416,6 @@
     seg = ext // SEGS
     lanes_count = lax.axis_size("tp")
     scaled = weights * jnp.sqrt(-jnp.expm1(-2.0 * rates))
-    apart = place - 1 - jnp.arange(count)
-    lags = jnp.where(apart >= 0, apart * rows - LEAD, -4 * LEAD).astype(f32)
-    lags = jnp.broadcast_to(lags[:, None], (count, 128))
     summed = -(-ext // 128) * 128
     col = lambda *lead: pl.BlockSpec(lead + (128,), lambda j: (0,) * len(lead) + (j,))
     groups = width // 128
@@ -445,7 +462,6 @@
             col(seg, SEGS),
             col(MODES, SEGS),
             pl.BlockSpec((1, count, MODES, 128), lambda j: (j, 0, 0, 0)),
-            full((count, 128)),
             col(win),
             col(ext - win),
             col(MODES),
@@ -456,7 +472,7 @@
         scratch_shapes=[pltpu.VMEM((MODES, SEGS, 128), f32), pltpu.VMEM((ext, 128), f32), pltpu.VMEM((MODES, 128), f32)],
         compiler_params=params(),
         name="mix",
-    )(prod, gate, states, totals, lags, near, far, rates, scaled)
+    )(prod, gate, states, totals, near, far, rates, scaled)
 
 
 def solution(mesh):

time: 78.5 us -> 95 us (1.21)
  Pallas kernels: 68.9 us -> 88.2 us
  local copies, waits for them, and re-layouts: 4.75 us -> 2.22 us
    pallas_call x0 -> x1, Pallas kernels: none -> 21 us  [body(): pl.pallas_call(functools.partial(tail_kernel, rows), in_specs=[anywhere,...]
    squeeze x2 -> x0, local copies, waits for them, and re-layouts: 1.85 us -> none  [the longest x1 1.09 us: body(): feats[1, rows - HALO:]]
    pallas_call x2, Pallas kernels: 25.3 us -> 23.8 us  [medium(): pl.pallas_call(functools.partial(first_kernel, rows, win, count_wins, beg...]
  transfers between devices with their start and end apart: 1 -> 1, of which waited for: 0 -> 0; matrix products, arithmetic and copies ran while one was open for 1% -> 2% of each run, Pallas kernels for 20% -> 16%
where the time goes in v1:
time: 95 us; the launch traced here: 94.5 us
  Pallas kernels  88.2 us (93%)
  starting transfers between devices  3.43 us (4%)
  local copies, waits for them, and re-layouts  2.22 us (2%)
    pallas_call x1, Pallas kernels, body(): pl.pallas_call(functools.partial(second_kernel, seg, count, lanes_count,...  29.8 us
    pallas_call x2, Pallas kernels, medium(): pl.pallas_call(functools.partial(first_kernel, rows, win, count_wins, beg...  23.8 us
    pallas_call x1, Pallas kernels, body(): pl.pallas_call(functools.partial(tail_kernel, rows), in_specs=[anywhere,...  21 us
    pallas_call x1, Pallas kernels, body(): pl.pallas_call(functools.partial(third_kernel, seg, count), grid=(width /...  13.6 us
    ppermute x1, starting transfers between devices, body(): halo = lax.ppermute(tail, 'ctx', [(i, i + 1) for i in range(count - 1)])  3.43 us
  transfers between devices with their start and end apart: 1, of which 0 were waited for; matrix products, arithmetic and copies ran while one was open for 2% of the time, Pallas kernels for 16%

profile of v1, /device:TPU:24, one launch (start us, length us, event | category | flops | bytes accessed | tf_op | source)
XLA Modules:
  0.0 94.5 jit_solution(10202855755449774089)
XLA Ops:
  0.0 21.0 %tail.1 = bf16[320,1024]{1,0:T(8,128)(2,1)} custom-call(bf16[3,1024,1024]{2,1,0:T(8,128)(2,1)} %bitcast.8, bf16[1024,1024]{1,0:T(8,128)(2,1)} %stream.5), custom_call_target="tpu_custom_call" | custom-call | tf_op jit(solution)/shard_map/tail/pallas_call | solution.py:358
  21.0 3.4 %collective-permute-start = (bf16[320,1024]{1,0:T(8,128)(2,1)}, bf16[320,1024]{1,0:T(8,128)(2,1)S(1)}, u32[]{:S(2)}, u32[]{:S(2)}) collective-permute-start(bf16[320,1024]{1,0:T(8,128)(2,1)} %tail.1), channel_id=1, source_target_pairs={{0,4},{4,8},{8,12},{12,16},{16,20},{20,24},{24,28},{1,5},{5,9},{9,... | collective-permute-start | bytes 1966088 | tf_op jit(solution)/shard_map/ppermute | solution.py:367
  24.4 1.4 %slice.3.halo = bf16[16,1024]{1,0:T(8,128)(2,1)} slice(bf16[1024,1024]{1,0:T(8,128)(2,1)} %stream.5), slice={[0:16], [0:1024]} | slice | bytes 65536 | tf_op jit(solution)/shard_map/slice | solution.py:414
  25.8 0.0 copy-start
  25.8 0.0 copy-start.1
  25.8 14.7 %medium_rest.1 = (f32[688,1024]{1,0:T(8,128)}, f32[688,128]{1,0:T(8,128)}) custom-call(bf16[3,1024,1024]{2,1,0:T(8,128)(2,1)} %bitcast.9, bf16[16,1024]{1,0:T(8,128)(2,1)} %slice.3.halo, bf16[1024,1024]{1,0:T(8,128)(2,1)} %stream.5, f32[3,7,1024]{2,1,0:T(8,128)} %bitcast.15, bf16[1024,128]{1,0:T(8,128)(2,1)} %filt.3, bf16[512,512]{1,0:T(8,128)(2,1)} %constant.8.clone.fh, ...), custom_call_target="tpu_custom_call" | custom-call | flops 24000000000 | bytes 40000000 | tf_op jit(solution)/shard_map/medium_rest/pallas_call | solution.py:381
  40.6 0.0 copy-done
  40.6 0.0 copy-done.1
  40.6 0.7 bitcast_multiply_fusion.weight
  41.2 0.0 collective-permute-done.halo
  41.3 0.0 copy-start.2
  41.3 0.8 copy-done.2
  42.1 9.0 %medium_head.1 = (f32[344,1024]{1,0:T(8,128)}, f32[344,128]{1,0:T(8,128)}) custom-call(bf16[3,1024,1024]{2,1,0:T(8,128)(2,1)} %bitcast.10, bf16[320,1024]{1,0:T(8,128)(2,1)} %copy-done.2, bf16[1024,1024]{1,0:T(8,128)(2,1)} %stream.5, f32[3,7,1024]{2,1,0:T(8,128)} %bitcast.16, bf16[1024,128]{1,0:T(8,128)(2,1)} %filt.3, bf16[512,512]{1,0:T(8,128)(2,1)} %constant.8.clone.fh, ...), custom_call_target="tpu_custom_call" | custom-call | flops 12000000000 | bytes 20000000 | tf_op jit(solution)/shard_map/medium_head/pallas_call | solution.py:381
  51.1 29.8 %states.1 = (f32[129,8,1024]{2,1,0:T(8,128)}, f32[129,8,1024]{2,1,0:T(8,128)}, f32[16,8,1024]{2,1,0:T(8,128)}, f32[8,8,16,128]{3,2,1,0:T(8,128)}) custom-call(f32[344,1024]{1,0:T(8,128)} %get-tuple-element.13.near, f32[688,1024]{1,0:T(8,128)} %get-tuple-element.14.far, f32[344,128]{1,0:T(8,128)} %get-tuple-element.15.near_sq, ...), custom_call_target="tpu_custom_call" | custom-call | tf_op jit(solution)/shard_map/states/pallas_call | solution.py:422
  80.9 13.6 %mix.1 = bf16[1024,1024]{1,0:T(8,128)(2,1)} custom-call(f32[129,8,1024]{2,1,0:T(8,128)} %get-tuple-element.17.prod, f32[129,8,1024]{2,1,0:T(8,128)} %get-tuple-element.18.gate, f32[16,8,1024]{2,1,0:T(8,128)} %get-tuple-element.19.states, f32[8,8,16,128]{3,2,1,0:T(8,128)} %get-tuple-element.20.totals, f32[344,1024]{1,0:T(8,128)} %get-tuple-element.13.near, ...), custom_call_target="tpu_custom_call" | custom-call | tf_op jit(solution)/shard_map/mix/pallas_call | solution.py:457
Async XLA Ops:
  21.0 20.3 %collective-permute-start = (bf16[320,1024]{1,0:T(8,128)(2,1)}, bf16[320,1024]{1,0:T(8,128)(2,1)S(1)}, u32[]{:S(2)}, u32[]{:S(2)}) collective-permute-start(bf16[320,1024]{1,0:T(8,128)(2,1)} %tail.1), channel_id=1, source_target_pairs={{0,4},{4,8},{8,12},{12,16},{16,20},{20,24},{24,28},{1,5},{5,9},{9,... | collective-permute-start | bytes 1966088 | tf_op jit(solution)/shard_map/ppermute | solution.py:367
  25.8 14.7 %copy-start = (f32[1024,16]{0,1:T(8,128)S(1)}, f32[1024,16]{0,1:T(8,128)}, u32[]{:S(2)}) copy-start(f32[1024,16]{0,1:T(8,128)} %param.17) | copy-start | bytes 196612
  25.8 14.8 %copy-start.1 = (f32[1024,16]{0,1:T(8,128)S(1)}, f32[1024,16]{0,1:T(8,128)}, u32[]{:S(2)}) copy-start(f32[1024,16]{0,1:T(8,128)} %param.18) | copy-start | bytes 196612
  41.3 0.8 copy-start.2

commit v2 on v1

--- a/solution.py
+++ b/solution.py
@@ -358,7 +358,7 @@
     tail = pl.pallas_call(
         functools.partial(tail_kernel, rows),
         in_specs=[anywhere, anywhere],
-        out_specs=anywhere,
+        out_specs=pl.BlockSpec(memory_space=pltpu.VMEM),
         out_shape=jax.ShapeDtypeStruct((2 * HALO + 32, width), bf16),
         scratch_shapes=[pltpu.SemaphoreType.DMA((4,))],
         compiler_params=pltpu.CompilerParams(vmem_limit_bytes=VMEM_LIMIT),
@@ -383,7 +383,7 @@
             grid=(width // cb,),
             in_specs=[
                 pl.BlockSpec((3, need, cb), lambda j: (0, 0, j)),
-                pl.BlockSpec((halo.shape[0], cb), lambda j: (0, j)),
+                pl.BlockSpec((halo.shape[0] if begin == 0 else 16, cb), lambda j: (0, j)),
                 pl.BlockSpec((need, cb), lambda j: (0, j)),
                 pl.BlockSpec((3, TAPS, cb), lambda j: (0, 0, j)),
                 pl.BlockSpec((cb, MR), lambda j: (j, 0)),
@@ -411,7 +411,7 @@
             name="medium_head" if begin == 0 else "medium_rest",
         )(feats, halo, stream_in, taps_one, mr_filter, fh, fl, g_mat)
 
-    far, far_squares = medium(win, wins - 1, stream_in[:16])
+    far, far_squares = medium(win, wins - 1, stream_in)
     near, near_squares = medium(0, 1, halo)
     seg = ext // SEGS
     lanes_count = lax.axis_size("tp")

time: 95 us -> 75.1 us (0.79)
  Pallas kernels: 88.2 us -> 69.1 us
  local copies, waits for them, and re-layouts: 2.22 us -> 0.85 us
    pallas_call x1, Pallas kernels: 21 us -> 1.92 us  [body(): pl.pallas_call(functools.partial(tail_kernel, rows), in_specs=[anywhere,...]
    slice x1 -> x0, local copies, waits for them, and re-layouts: 1.38 us -> none  [body(): far, far_squares = medium(win, wins - 1, stream_in[:16])]
  transfers between devices with their start and end apart: 1 -> 1, of which waited for: 0 -> 1; matrix products, arithmetic and copies ran while one was open for 2% -> 1% of each run, Pallas kernels for 16% -> 20%
where the time goes in v2:
time: 75.1 us; the launch traced here: 74.7 us
  Pallas kernels  69.1 us (92%)
  starting transfers between devices  3.43 us (5%)
  local copies, waits for them, and re-layouts  0.85 us (1%)
    pallas_call x1, Pallas kernels, body(): pl.pallas_call(functools.partial(second_kernel, seg, count, lanes_count,...  29.9 us
    pallas_call x2, Pallas kernels, medium(): pl.pallas_call(functools.partial(first_kernel, rows, win, count_wins, beg...  23.8 us
    pallas_call x1, Pallas kernels, body(): pl.pallas_call(functools.partial(third_kernel, seg, count), grid=(width /...  13.6 us
    ppermute x1, starting transfers between devices, body(): halo = lax.ppermute(tail, 'ctx', [(i, i + 1) for i in range(count - 1)])  3.43 us
    pallas_call x1, Pallas kernels, body(): pl.pallas_call(functools.partial(tail_kernel, rows), in_specs=[anywhere,...  1.92 us
  transfers between devices with their start and end apart: 1, of which 1 were waited for; matrix products, arithmetic and copies ran while one was open for 1% of the time, Pallas kernels for 20%

profile of v2, /device:TPU:24, one launch (start us, length us, event | category | flops | bytes accessed | tf_op | source)
XLA Modules:
  0.0 74.7 jit_solution(5124982869887438867)
XLA Ops:
  0.0 1.9 %tail.1 = bf16[320,1024]{1,0:T(8,128)(2,1)} custom-call(bf16[3,1024,1024]{2,1,0:T(8,128)(2,1)} %bitcast.8, bf16[1024,1024]{1,0:T(8,128)(2,1)} %stream.5), custom_call_target="tpu_custom_call" | custom-call | tf_op jit(solution)/shard_map/tail/pallas_call | solution.py:358
  1.9 3.4 %collective-permute-start = (bf16[320,1024]{1,0:T(8,128)(2,1)}, bf16[320,1024]{1,0:T(8,128)(2,1)S(1)}, u32[]{:S(2)}, u32[]{:S(2)}) collective-permute-start(bf16[320,1024]{1,0:T(8,128)(2,1)} %tail.1), channel_id=1, source_target_pairs={{0,4},{4,8},{8,12},{12,16},{16,20},{20,24},{24,28},{1,5},{5,9},{9,... | collective-permute-start | bytes 1966088 | tf_op jit(solution)/shard_map/ppermute | solution.py:367
  5.4 0.0 copy-start
  5.4 0.0 copy-start.1
  5.4 14.8 %medium_rest.1 = (f32[688,1024]{1,0:T(8,128)}, f32[688,128]{1,0:T(8,128)}) custom-call(bf16[3,1024,1024]{2,1,0:T(8,128)(2,1)} %bitcast.9, bf16[1024,1024]{1,0:T(8,128)(2,1)} %stream.5, bf16[1024,1024]{1,0:T(8,128)(2,1)} %stream.5, f32[3,7,1024]{2,1,0:T(8,128)} %bitcast.15, bf16[1024,128]{1,0:T(8,128)(2,1)} %filt.3, bf16[512,512]{1,0:T(8,128)(2,1)} %constant.8.clone.fh, ...), custom_call_target="tpu_custom_call" | custom-call | flops 24000000000 | bytes 40000000 | tf_op jit(solution)/shard_map/medium_rest/pallas_call | solution.py:381
  20.2 0.0 copy-done
  20.2 0.0 copy-done.1
  20.2 0.7 bitcast_multiply_fusion.weight
  20.8 0.6 collective-permute-done.halo
  21.4 0.0 copy-start.2
  21.4 0.8 %copy-done.2 = bf16[320,1024]{1,0:T(8,128)(2,1)} copy-done((bf16[320,1024]{1,0:T(8,128)(2,1)}, bf16[320,1024]{1,0:T(8,128)(2,1)S(1)}, u32[]{:S(2)}) %copy-start.2) | copy-done | bytes 655384
  22.2 9.0 %medium_head.1 = (f32[344,1024]{1,0:T(8,128)}, f32[344,128]{1,0:T(8,128)}) custom-call(bf16[3,1024,1024]{2,1,0:T(8,128)(2,1)} %bitcast.10, bf16[320,1024]{1,0:T(8,128)(2,1)} %copy-done.2, bf16[1024,1024]{1,0:T(8,128)(2,1)} %stream.5, f32[3,7,1024]{2,1,0:T(8,128)} %bitcast.16, bf16[1024,128]{1,0:T(8,128)(2,1)} %filt.3, bf16[512,512]{1,0:T(8,128)(2,1)} %constant.8.clone.fh, ...), custom_call_target="tpu_custom_call" | custom-call | flops 12000000000 | bytes 20000000 | tf_op jit(solution)/shard_map/medium_head/pallas_call | solution.py:381
  31.2 29.9 %states.1 = (f32[129,8,1024]{2,1,0:T(8,128)}, f32[129,8,1024]{2,1,0:T(8,128)}, f32[16,8,1024]{2,1,0:T(8,128)}, f32[8,8,16,128]{3,2,1,0:T(8,128)}) custom-call(f32[344,1024]{1,0:T(8,128)} %get-tuple-element.13.near, f32[688,1024]{1,0:T(8,128)} %get-tuple-element.14.far, f32[344,128]{1,0:T(8,128)} %get-tuple-element.15.near_sq, ...), custom_call_target="tpu_custom_call" | custom-call | tf_op jit(solution)/shard_map/states/pallas_call | solution.py:422
  61.1 13.6 %mix.1 = bf16[1024,1024]{1,0:T(8,128)(2,1)} custom-call(f32[129,8,1024]{2,1,0:T(8,128)} %get-tuple-element.17.prod, f32[129,8,1024]{2,1,0:T(8,128)} %get-tuple-element.18.gate, f32[16,8,1024]{2,1,0:T(8,128)} %get-tuple-element.19.states, f32[8,8,16,128]{3,2,1,0:T(8,128)} %get-tuple-element.20.totals, f32[344,1024]{1,0:T(8,128)} %get-tuple-element.13.near, ...), custom_call_target="tpu_custom_call" | custom-call | tf_op jit(solution)/shard_map/mix/pallas_call | solution.py:457
Async XLA Ops:
  1.9 19.5 %collective-permute-start = (bf16[320,1024]{1,0:T(8,128)(2,1)}, bf16[320,1024]{1,0:T(8,128)(2,1)S(1)}, u32[]{:S(2)}, u32[]{:S(2)}) collective-permute-start(bf16[320,1024]{1,0:T(8,128)(2,1)} %tail.1), channel_id=1, source_target_pairs={{0,4},{4,8},{8,12},{12,16},{16,20},{20,24},{24,28},{1,5},{5,9},{9,... | collective-permute-start | bytes 1966088 | tf_op jit(solution)/shard_map/ppermute | solution.py:367
  5.4 14.8 %copy-start = (f32[1024,16]{0,1:T(8,128)S(1)}, f32[1024,16]{0,1:T(8,128)}, u32[]{:S(2)}) copy-start(f32[1024,16]{0,1:T(8,128)} %param.17) | copy-start | bytes 196612
  5.4 14.8 %copy-start.1 = (f32[1024,16]{0,1:T(8,128)S(1)}, f32[1024,16]{0,1:T(8,128)}, u32[]{:S(2)}) copy-start(f32[1024,16]{0,1:T(8,128)} %param.18) | copy-start | bytes 196612
  21.4 0.8 %copy-start.2 = (bf16[320,1024]{1,0:T(8,128)(2,1)}, bf16[320,1024]{1,0:T(8,128)(2,1)S(1)}, u32[]{:S(2)}) copy-start(bf16[320,1024]{1,0:T(8,128)(2,1)S(1)} %collective-permute-done.halo) | copy-start | bytes 1966084
